TPU v7x, 32 devices: a whole 2x2x4 slice. The times are simulated.
32 devices in a mesh: groups: 2 (over x), expert: 16 (over z, y, core).
Axes of the slice: x: 2, y: 2, z: 4, core: 2. Of those that a mesh axis runs over, the one named last changes fastest.
Arguments:
- tokens: bfloat16 [4096, 4096], P(('groups', 'expert')), parts along dimension 0, may hold values from -6 to 6
- cotangent: bfloat16 [4096, 4096], P(('groups', 'expert')), parts along dimension 0, may hold values from -0.29882812 to 0.29882812
- gate_prob: bfloat16 [4096], P(('groups', 'expert')), parts along dimension 0, may hold values from 0.29882812 to 1
- experts_of: int32 [4096, 1], P(('groups', 'expert')), parts along dimension 0, may hold values from 0 to 15; in each aligned block of 128 rows (0 to 127, 128 to 255, ...) at most 10 rows name the same one
- in_weight: bfloat16 [40960, 4096], P('expert'), may hold values from -0.09375 to 0.09375
- out_weight: bfloat16 [40960, 4096], P('expert'), may hold values from -0.125 to 0.125
Outputs:
- gate_grad: float32 [4096], P(('groups', 'expert')), parts along dimension 0
- in_grad: bfloat16 [81920, 4096], P(('groups', 'expert')), parts along dimension 0
- out_grad: bfloat16 [81920, 4096], P(('groups', 'expert')), parts along dimension 0
There are 2 independent parts, one for each index of `groups`. A program takes and returns all parts, laid end to end along the dimension named above; an argument that names none is the same for every part. Nothing has to cross between parts.
Inputs may be any that keep to these rules, and one draw needn't show every extreme that they name: `experts_of`: among the rows of one device no expert is named more than 10 times, and in some device's rows one expert is named exactly 10 times.
All inputs are finite; a program needn't handle non-finite values.
Results may differ from a plain program's by a relative error of at most 0.011.
Values may be sent and summed in bfloat16 or wider, within the bound.
A program may use at most 192 MiB of HBM per device.

v0:
```python
import jax
import jax.numpy as jnp
from jax import lax
from jax.sharding import PartitionSpec as P

EXPERTS = 16


def contract_last(left, right):
    return lax.dot_general(
        left, right, (((1,), (1,)), ((), ())), preferred_element_type=jnp.float32
    )


def expert_rows(rows_tok, rows_grad, rows_gate, weight_in, weight_out):
    preact = contract_last(weight_in, rows_tok)
    hidden = jnp.maximum(preact, 0.0).astype(jnp.bfloat16)
    back = contract_last(weight_out, rows_grad)
    gate_part = jnp.sum(hidden.astype(jnp.float32) * back, axis=0)
    gate_wide = rows_gate.astype(jnp.float32)
    hidden_grad = jnp.where(preact > 0, gate_wide[None, :] * back, 0.0).astype(jnp.bfloat16)
    scaled = (gate_wide[:, None] * rows_grad.astype(jnp.float32)).astype(jnp.bfloat16)
    grad_out = jnp.dot(hidden, scaled, preferred_element_type=jnp.float32)
    grad_in = jnp.dot(hidden_grad, rows_tok, preferred_element_type=jnp.float32)
    return (grad_in, grad_out, gate_part)


def run_pass(rows_tok, rows_grad, rows_gate, live, weight_in, weight_out):
    keep_wide = live.astype(jnp.float32)
    masked_gate = jnp.where(live > 0, rows_gate, 0.0)
    grad_in, grad_out, part = expert_rows(rows_tok, rows_grad, masked_gate, weight_in, weight_out)
    return (grad_in, grad_out, part * keep_wide)


def per_device(tokens, cotangent, gate_prob, experts_of, in_weight, out_weight):
    devices = lax.axis_size("expert")
    groups = EXPERTS
    slabs = devices // groups
    count_tok = tokens.shape[0]
    width = tokens.shape[1]
    capacity = 5 * count_tok // (4 * groups)
    chosen = experts_of[:, 0]
    labels = jnp.arange(groups, dtype=jnp.int32)
    onehot = (chosen[:, None] == labels[None, :]).astype(jnp.int32)
    place = jnp.sum((jnp.cumsum(onehot, axis=0) - 1) * onehot, axis=1)
    moved = jnp.zeros((count_tok,), jnp.bool_)
    code = chosen * capacity + place
    table = jnp.arange(groups * capacity, dtype=jnp.int32)[:, None] == code[None, :]
    selector = table.astype(jnp.bfloat16)
    signed_gate = jnp.where(moved, -gate_prob.astype(jnp.float32), gate_prob.astype(jnp.float32))
    packed_tok = (
        jnp.dot(selector, tokens, preferred_element_type=jnp.float32)
        .astype(jnp.bfloat16)
        .reshape(groups, capacity, width)
    )
    packed_grad = (
        jnp.dot(selector, cotangent, preferred_element_type=jnp.float32)
        .astype(jnp.bfloat16)
        .reshape(groups, capacity, width)
    )
    packed_gate = (
        jnp.sum(jnp.where(table, signed_gate[None, :], 0.0), axis=1)
        .astype(jnp.bfloat16)
        .reshape(groups, capacity)
    )

    def spread(values):
        shaped = values[:, None]
        widened = jnp.broadcast_to(shaped, (groups, slabs) + values.shape[1:])
        return widened.reshape((devices,) + values.shape[1:])

    arrived_tok, arrived_grad, arrived_gate = (
        lax.all_to_all(spread(packed_tok), "expert", split_axis=0, concat_axis=0, tiled=True),
        lax.all_to_all(spread(packed_grad), "expert", split_axis=0, concat_axis=0, tiled=True),
        lax.all_to_all(spread(packed_gate), "expert", split_axis=0, concat_axis=0, tiled=True),
    )
    rows_tok = arrived_tok.reshape(devices * capacity, width)
    rows_grad = arrived_grad.reshape(devices * capacity, width)
    rows_signed = arrived_gate.reshape(devices * capacity)
    rows_gate = jnp.abs(rows_signed)
    present = (rows_signed != 0).astype(jnp.int32)
    grad_in, grad_out, gate_part = run_pass(
        rows_tok, rows_grad, rows_gate, present, in_weight, out_weight
    )
    source_parts = gate_part.reshape(devices, capacity)
    back_terms = lax.all_to_all(source_parts, "expert", split_axis=0, concat_axis=0, tiled=True)
    summed = jnp.sum(back_terms.reshape(groups, slabs, capacity), axis=1).reshape(groups * capacity)
    gate_grad = jnp.sum(jnp.where(table, summed[:, None], 0.0), axis=0)
    return (gate_grad, grad_in.astype(jnp.bfloat16), grad_out.astype(jnp.bfloat16))


def solution(mesh):
    return jax.shard_map(
        per_device,
        mesh=mesh,
        in_specs=(
            P(("groups", "expert"), None),
            P(("groups", "expert"), None),
            P(("groups", "expert")),
            P(("groups", "expert"), None),
            P("expert", None),
            P("expert", None),
        ),
        out_specs=(
            P(("groups", "expert")),
            P(("groups", "expert"), None),
            P(("groups", "expert"), None),
        ),
        check_vma=False,
    )
```

profile of v0, /device:TPU:0, one launch (start us, length us, event | category | flops | bytes accessed | tf_op | source)
XLA Modules:
  0.0 167.3 jit_solution(409431124934563286)
XLA Ops:
  0.6 0.7 convert_element_type.88
  1.4 0.7 fusion.3
  2.3 0.8 select_reduce_fusion.2
  3.1 0.7 multiply_add_fusion
  3.9 0.7 convert_element_type.101
  4.6 7.4 %all-to-all-start.2 = ((bf16[16,1,10]{2,1,0:T(2,128)(2,1)}), bf16[16,1,10]{2,1,0:T(2,128)(2,1)S(1)}, u32[]{:S(2)}, u32[]{:S(2)}) async-start(bf16[16,1,10]{2,1,0:T(2,128)(2,1)} %convert_element_type.101), calls=%async_computation.2 | async-start | bytes 16384 | tf_op jit(solution)/shard_map/all_to_all | solution.py:75
  12.5 1.6 reshape_broadcast_in_dim_reshape.7
  14.1 4.3 %all-to-all-done.2 = bf16[16,1,10]{2,1,0:T(2,128)(2,1)S(1)} async-done(((bf16[16,1,10]{2,1,0:T(2,128)(2,1)}), bf16[16,1,10]{2,1,0:T(2,128)(2,1)S(1)}, u32[]{:S(2)}, u32[]{:S(2)}) %all-to-all-start.2) | async-done | bytes 352 | tf_op jit(solution)/shard_map/all_to_all | solution.py:75
  18.4 3.7 %all-to-all-start = ((bf16[16,10,4096]{2,1,0:T(8,128)(2,1)}), bf16[16,10,4096]{2,1,0:T(8,128)(2,1)S(1)}, u32[]{:S(2)}, u32[]{:S(2)}) async-start(bf16[16,10,4096]{2,1,0:T(8,128)(2,1)} %reshape_broadcast_in_dim_reshape.7), calls=%async_computation | async-start | bytes 4194304 | tf_op jit(solution)/shard_map/all_to_all | solution.py:73
  22.1 1.6 convolution_convert_fusion.2
  23.7 2.6 %reshape_broadcast_in_dim_reshape.8 = bf16[16,10,4096]{2,1,0:T(8,128)(2,1)} reshape(bf16[160,4096]{1,0:T(8,128)(2,1)} %convolution_convert_fusion.2) | data formatting | bytes 2621440 | tf_op jit(solution)/shard_map/reshape;broadcast_in_dim;reshape | solution.py:70
  26.3 36.8 %all-to-all-done = bf16[16,10,4096]{2,1,0:T(8,128)(2,1)S(1)} async-done(((bf16[16,10,4096]{2,1,0:T(8,128)(2,1)}), bf16[16,10,4096]{2,1,0:T(8,128)(2,1)S(1)}, u32[]{:S(2)}, u32[]{:S(2)}) %all-to-all-start) | async-done | bytes 1310752 | tf_op jit(solution)/shard_map/all_to_all | solution.py:73
  63.1 11.2 %all-to-all-start.1 = ((bf16[16,10,4096]{2,1,0:T(8,128)(2,1)}), bf16[16,10,4096]{2,1,0:T(8,128)(2,1)}, u32[]{:S(2)}, u32[]{:S(2)}) async-start(bf16[16,10,4096]{2,1,0:T(8,128)(2,1)} %reshape_broadcast_in_dim_reshape.8), calls=%async_computation.1 | async-start | bytes 4194304 | tf_op jit(solution)/shard_map/all_to_all | solution.py:74
  74.5 1.4 reshape.83
  75.8 11.5 %fusion.11 = f32[160,2560]{1,0:T(8,128)S(1)} fusion(bf16[160,4096]{1,0:T(8,128)(2,1)} %reshape.83, bf16[2560,4096]{1,0:T(8,128)(2,1)} %param.10), kind=kOutput, calls=%fused_computation.27 | convolution fusion | flops 3355443200 | bytes 23920640 | tf_op jit(solution)/shard_map/dot_general | solution.py:10
  87.4 28.2 %all-to-all-done.1 = bf16[16,10,4096]{2,1,0:T(8,128)(2,1)} async-done(((bf16[16,10,4096]{2,1,0:T(8,128)(2,1)}), bf16[16,10,4096]{2,1,0:T(8,128)(2,1)}, u32[]{:S(2)}, u32[]{:S(2)}) %all-to-all-start.1) | async-done | bytes 1310752 | tf_op jit(solution)/shard_map/all_to_all | solution.py:74
  115.5 2.6 %reshape.84 = bf16[160,4096]{1,0:T(8,128)(2,1)} reshape(bf16[16,10,4096]{2,1,0:T(8,128)(2,1)} %all-to-all-done.1) | data formatting | bytes 2621440 | tf_op jit(solution)/shard_map/reshape | solution.py:78
  118.1 12.5 %multiply_reduce_fusion = (f32[160]{0:T(256)S(1)}, f32[160,2560]{1,0:T(8,128)}) fusion(f32[160,2560]{1,0:T(8,128)S(1)} %fusion.11, bf16[160,4096]{1,0:T(8,128)(2,1)} %reshape.84, bf16[2560,4096]{1,0:T(8,128)(2,1)} %param.11), kind=kOutput, calls=%fused_computation.6 | convolution fusion | flops 3357081344 | bytes 25559680 | tf_op jit(solution)/shard_map/dot_general | solution.py:10
  130.8 0.6 fusion.6
  131.4 11.2 %all-to-all-start.3 = ((f32[16,1,10]{2,1,0:T(1,128)}), f32[16,1,10]{2,1,0:T(1,128)S(1)}, u32[]{:S(2)}, u32[]{:S(2)}) async-start(f32[16,1,10]{2,1,0:T(1,128)} %bitcast.1), calls=%async_computation.3 | async-start | bytes 16384 | tf_op jit(solution)/shard_map/all_to_all | solution.py:86
  142.6 12.2 %convolution_convert_fusion.1 = bf16[2560,4096]{1,0:T(8,128)(2,1)} fusion(bf16[160,4096]{1,0:T(8,128)(2,1)} %reshape.83, f32[160,2560]{1,0:T(8,128)} %get-tuple-element.4, f32[160,2560]{1,0:T(8,128)S(1)} %fusion.11, f32[160]{0:T(256)S(1)} %reshape.85), kind=kOutput, calls=%fused_computation.1 | convolution fusion | flops 3367567360 | bytes 25559680 | tf_op jit(solution)/shard_map/dot_general | solution.py:24
  154.8 10.6 %convolution_convert_fusion = bf16[2560,4096]{1,0:T(8,128)(2,1)} fusion(bf16[160,4096]{1,0:T(8,128)(2,1)S(1)} %copy-done.2, f32[160]{0:T(256)S(1)} %reshape.85, f32[160,2560]{1,0:T(8,128)S(1)} %fusion.11), kind=kOutput, calls=%fused_computation | convolution fusion | flops 3368714240 | bytes 23921280 | tf_op jit(solution)/shard_map/dot_general | solution.py:23
  165.9 0.7 reduce.4
  166.7 0.6 select_reduce_fusion
  (17 shorter events, 1.6 us)
Async XLA Ops:
  0.6 11.4 %copy-start = (bf16[128,4096]{1,0:T(8,128)(2,1)S(1)}, bf16[128,4096]{1,0:T(8,128)(2,1)}, u32[]{:S(2)}) copy-start(bf16[128,4096]{1,0:T(8,128)(2,1)} %param.6) | copy-start | bytes 3145732
  4.6 13.7 %all-to-all-start.2 = ((bf16[16,1,10]{2,1,0:T(2,128)(2,1)}), bf16[16,1,10]{2,1,0:T(2,128)(2,1)S(1)}, u32[]{:S(2)}, u32[]{:S(2)}) async-start(bf16[16,1,10]{2,1,0:T(2,128)(2,1)} %convert_element_type.101), calls=%async_computation.2 | async-start | bytes 16384 | tf_op jit(solution)/shard_map/all_to_all | solution.py:75
  14.1 8.0 %copy-start.3 = (bf16[128,4096]{1,0:T(8,128)(2,1)S(1)}, bf16[128,4096]{1,0:T(8,128)(2,1)}, u32[]{:S(2)}) copy-start(bf16[128,4096]{1,0:T(8,128)(2,1)} %param.7) | copy-start | bytes 3145732
  18.4 44.8 %all-to-all-start = ((bf16[16,10,4096]{2,1,0:T(8,128)(2,1)}), bf16[16,10,4096]{2,1,0:T(8,128)(2,1)S(1)}, u32[]{:S(2)}, u32[]{:S(2)}) async-start(bf16[16,10,4096]{2,1,0:T(8,128)(2,1)} %reshape_broadcast_in_dim_reshape.7), calls=%async_computation | async-start | bytes 4194304 | tf_op jit(solution)/shard_map/all_to_all | solution.py:73
  63.1 52.4 %all-to-all-start.1 = ((bf16[16,10,4096]{2,1,0:T(8,128)(2,1)}), bf16[16,10,4096]{2,1,0:T(8,128)(2,1)}, u32[]{:S(2)}, u32[]{:S(2)}) async-start(bf16[16,10,4096]{2,1,0:T(8,128)(2,1)} %reshape_broadcast_in_dim_reshape.8), calls=%async_computation.1 | async-start | bytes 4194304 | tf_op jit(solution)/shard_map/all_to_all | solution.py:74
  131.4 34.0 %all-to-all-start.3 = ((f32[16,1,10]{2,1,0:T(1,128)}), f32[16,1,10]{2,1,0:T(1,128)S(1)}, u32[]{:S(2)}, u32[]{:S(2)}) async-start(f32[16,1,10]{2,1,0:T(1,128)} %bitcast.1), calls=%async_computation.3 | async-start | bytes 16384 | tf_op jit(solution)/shard_map/all_to_all | solution.py:86
  142.6 12.2 %copy-start.2 = (bf16[160,4096]{1,0:T(8,128)(2,1)S(1)}, bf16[160,4096]{1,0:T(8,128)(2,1)}, u32[]{:S(2)}) copy-start(bf16[160,4096]{1,0:T(8,128)(2,1)} %reshape.84) | copy-start | bytes 3932164
  154.8 12.5 %copy-start.1 = (bf16[128,4096]{1,0:T(8,128)(2,1)S(1)}, bf16[128,4096]{1,0:T(8,128)(2,1)}, u32[]{:S(2)}) copy-start(bf16[128,4096]{1,0:T(8,128)(2,1)} %param.6) | copy-start | bytes 3145732
where the time goes:
time: 168 us; the launch traced here: 167 us
  waiting for transfers between devices  69.3 us (41%)
  matrix products  48.9 us (29%)
  starting transfers between devices  33.6 us (20%)
  local copies, waits for them, and re-layouts  9.63 us (6%)
  other arithmetic  5.17 us (3%)
    all_to_all x1, waiting for transfers between devices, per_device(): lax.all_to_all(spread(packed_tok), 'expert', split_axis=0, concat_axis=0,...  36.8 us
    all_to_all x1, waiting for transfers between devices, per_device(): lax.all_to_all(spread(packed_grad), 'expert', split_axis=0, concat_axis=0...  28.2 us
    dot_general x2, matrix products, contract_last(): lax.dot_general(left, right, (((1,), (1,)), ((), ())), preferred_element_...  24.1 us
    dot_general x1, matrix products, expert_rows(): grad_in = jnp.dot(hidden_grad, rows_tok, preferred_element_type=jnp.float32)  12.2 us
    all_to_all x1, starting transfers between devices, per_device(): lax.all_to_all(spread(packed_grad), 'expert', split_axis=0, concat_axis=0...  11.2 us
    all_to_all x1, starting transfers between devices, per_device(): lax.all_to_all(source_parts, 'expert', split_axis=0, concat_axis=0, tiled...  11.2 us
    dot_general x1, matrix products, expert_rows(): grad_out = jnp.dot(hidden, scaled, preferred_element_type=jnp.float32)  10.6 us
    all_to_all x1, starting transfers between devices, per_device(): lax.all_to_all(spread(packed_gate), 'expert', split_axis=0, concat_axis=0...  7.39 us
  transfers between devices with their start and end apart: 4, of which 3 were waited for; matrix products, arithmetic and copies ran while one was open for 25% of the time, Pallas kernels for 0%

commit v1 on v0

v1 whole, which is shorter than its diff:
```python
import functools
import math

import jax
import jax.numpy as jnp
from jax import lax
from jax.experimental import pallas as pl
from jax.experimental.pallas import tpu as pltpu
from jax.sharding import PartitionSpec as P

EXPERTS = 16
SUB = 16
PARTS = 4
MESH = pl.DeviceIdType.MESH
BF = jnp.bfloat16
F32 = jnp.float32


def contract_last(left, right):
    return lax.dot_general(
        left, right, (((1,), (1,)), ((), ())), preferred_element_type=F32
    )


def mm(left, right):
    return jnp.dot(left, right, preferred_element_type=F32)


def iota(shape, dim):
    return lax.broadcasted_iota(jnp.int32, shape, dim)


def hot(cond):
    return jnp.where(cond, 1.0, 0.0).astype(BF)


def exchange(
    n, slabs, cap,
    tok, cot, gate, who, w_in, w_out,
    gate_grad, hid_out, hg_out, tok_out, sc_out,
    stage, send_b, send_a, recv_b, recv_a, win, wout, pre, back,
    stg_tok, stg_sc, ret_s, ret_r,
    in_sem, w_sem, send_sem, recv_sem, out_sem, ret_sem,
):
    me = lax.axis_index("expert")
    count = tok.shape[0]
    chunk = stage.shape[1] // PARTS
    extra = SUB - cap
    rest = cap - extra
    rows = EXPERTS * SUB
    total = n * SUB
    ffn = w_in.shape[0]
    tile = math.gcd(ffn, 512)
    block = 256

    barrier = pltpu.get_barrier_semaphore()

    @pl.loop(1, n)
    def _(i):
        pl.semaphore_signal(
            barrier, inc=1, device_id={"expert": lax.rem(me + i, n)}, device_id_type=MESH
        )

    ins = [
        pltpu.make_async_copy(cot, stage.at[pl.ds(count, count)], in_sem.at[0]),
        pltpu.make_async_copy(tok, stage.at[pl.ds(0, count)], in_sem.at[1]),
    ]
    for c in ins:
        c.start()

    def weights(k):
        cols = pl.ds(k * chunk, chunk)
        return [
            pltpu.make_async_copy(w_in.at[:, cols], win.at[k % 2], w_sem.at[0, k % 2]),
            pltpu.make_async_copy(w_out.at[:, cols], wout.at[k % 2], w_sem.at[1, k % 2]),
        ]

    loads = [weights(k) for k in range(PARTS)]

    chosen = who[...]
    square = (count, count)
    chosen_col = jnp.transpose(jnp.broadcast_to(chosen.astype(F32), square)).astype(jnp.int32)
    earlier = (chosen_col == chosen) & (iota(square, 0) < iota(square, 1))
    place = jnp.sum(jnp.where(earlier, 1.0, 0.0), axis=0, keepdims=True)
    place_col = jnp.transpose(jnp.broadcast_to(place, square)).astype(jnp.int32)
    code = jnp.broadcast_to(chosen * SUB + place.astype(jnp.int32), (rows, count))
    row = iota((rows, count), 0)
    slot = row % SUB
    sel_tok = (code == row) & (slot < cap)
    sel_cot = (code == row - cap) & (slot >= cap)
    sel = jnp.concatenate([hot(sel_tok), hot(sel_cot)], axis=1)
    gates = jnp.sum(
        jnp.where(sel_tok, jnp.broadcast_to(gate[...].astype(F32), (rows, count)), 0.0),
        axis=1, keepdims=True,
    )
    send_b[:, pl.ds(chunk, 128)] = jnp.broadcast_to(gates, (rows, 128)).astype(BF)
    ins[0].wait()
    late = jnp.zeros((rows, chunk), F32)
    for q in range(PARTS):
        pick = hot((slot % PARTS == q) & (code == row - slot + extra + slot // PARTS))
        late = late + mm(pick, stage[pl.ds(count, count), pl.ds(q * chunk, chunk)])
    send_b[:, pl.ds(0, chunk)] = late.astype(BF)
    ins[1].wait()

    pl.semaphore_wait(barrier, n - 1)

    def send(src, dst, at):
        @pl.loop(1, n)
        def _(i):
            to = lax.rem(me + i, n)
            pltpu.make_async_remote_copy(
                src_ref=src.at[pl.ds(pl.multiple_of(to // slabs * SUB, SUB), SUB)],
                dst_ref=dst.at[pl.ds(pl.multiple_of(me * SUB, SUB), SUB)],
                send_sem=send_sem.at[at],
                recv_sem=recv_sem.at[at],
                device_id={"expert": to},
                device_id_type=MESH,
            ).start()

        dst[pl.ds(pl.multiple_of(me * SUB, SUB), SUB), :] = src[
            pl.ds(pl.multiple_of(me // slabs * SUB, SUB), SUB), :
        ]

    def arrived(dst, at):
        part = dst.at[pl.ds(0, total - SUB)]
        pltpu.make_async_copy(part, part, recv_sem.at[at]).wait()

    def left(dst, at):
        part = dst.at[pl.ds(0, total - SUB)]
        pltpu.make_async_copy(part, part, send_sem.at[at]).wait()

    send(send_b, recv_b, PARTS)
    for k in range(PARTS):
        send_a[k] = mm(sel, stage[:, pl.ds(k * chunk, chunk)]).astype(BF)
        send(send_a.at[k], recv_a.at[k], k)
    for k in range(2):
        for c in loads[k]:
            c.start()

    arrived(recv_b, PARTS)
    lane0 = hot(iota((8, 128), 1) == 0)
    gate_row = contract_last(lane0, recv_b[:, pl.ds(chunk, 128)])[0:1]

    def outs(k):
        cols = pl.ds(k * chunk, chunk)
        return [
            pltpu.make_async_copy(stg_tok.at[k % 2], tok_out.at[:, cols], out_sem.at[0, k % 2]),
            pltpu.make_async_copy(stg_sc.at[k % 2], sc_out.at[:, cols], out_sem.at[1, k % 2]),
        ]

    writes = [outs(k) for k in range(PARTS)]
    r0 = iota((block, block), 0)
    r1 = iota((block, block), 1)
    j = r0 % SUB
    keep = hot((r0 == r1) & (j < cap))
    first = hot((r1 == r0 + cap) & (j < extra))
    part_sum = jnp.zeros((8, total), F32)
    for k in range(PARTS):
        for c in loads[k]:
            c.wait()
        if k >= 2:
            for c in writes[k - 2]:
                c.wait()
        arrived(recv_a.at[k], k)
        second = hot((j >= extra) & (j < cap) & (r1 == r0 - j + (j - extra) * PARTS + k))

        @pl.loop(0, total // block)
        def _(b):
            at = pl.ds(pl.multiple_of(b * block, block), block)
            mixed = recv_a[k, at, :]
            gate_col = recv_b[at, pl.ds(chunk, 128)].astype(F32)[:, 0:1]
            stg_tok[k % 2, at, :] = mm(keep, mixed).astype(BF)
            grads = mm(first, mixed) + mm(second, recv_b[at, pl.ds(0, chunk)])
            recv_a[k, at, :] = grads.astype(BF)
            stg_sc[k % 2, at, :] = (gate_col * grads).astype(BF)

        for c in writes[k]:
            c.start()

        def step(i, acc):
            at = pl.ds(pl.multiple_of(i * tile, tile), tile)
            p = contract_last(win[k % 2, at, :], stg_tok[k % 2])
            g = contract_last(wout[k % 2, at, :], recv_a[k])
            if k > 0:
                p = p + pre[at, :]
                g = g + back[at, :]
            if k < PARTS - 1:
                pre[at, :] = p
                back[at, :] = g
                return acc
            hidden = jnp.maximum(p, 0.0).astype(BF)
            hid_out[at, :] = hidden
            hg_out[at, :] = jnp.where(p > 0, gate_row * g, 0.0).astype(BF)
            share = hidden.astype(F32) * g
            return acc + jnp.sum(share.reshape(tile // 8, 8, total), axis=0)

        part_sum = lax.fori_loop(0, ffn // tile, step, part_sum)
        if k + 2 < PARTS:
            for c in loads[k + 2]:
                c.start()

    shares = jnp.sum(part_sum, axis=0, keepdims=True)
    per_tile = 128 // SUB
    for h in range(total // 128):
        ret_s[h] = jnp.broadcast_to(shares[:, h * 128:(h + 1) * 128], (8, 128))

    @pl.loop(1, n)
    def _(i):
        to = lax.rem(me + i, n)
        pltpu.make_async_remote_copy(
            src_ref=ret_s.at[to // per_tile],
            dst_ref=ret_r.at[me],
            send_sem=ret_sem.at[0],
            recv_sem=ret_sem.at[1],
            device_id={"expert": to},
            device_id_type=MESH,
        ).start()

    ret_r[me] = ret_s[me // per_tile]
    for k in range(PARTS - 2, PARTS):
        for c in writes[k]:
            c.wait()
    for k in range(PARTS):
        left(recv_a.at[k], k)
    left(recv_b, PARTS)
    tail = ret_r.at[pl.ds(0, n - 1)]
    for s in range(2):
        pltpu.make_async_copy(tail, tail, ret_sem.at[s]).wait()

    found = jnp.zeros((count, 128), F32)
    for d in range(n):
        found = found + jnp.where(chosen_col == d // slabs, ret_r[d][0:1], 0.0)
    mine = iota((count, 128), 1) == place_col + SUB * lax.rem(me, per_tile)
    column = jnp.sum(jnp.where(mine, found, 0.0), axis=1, keepdims=True)
    gate_grad[...] = jnp.transpose(jnp.broadcast_to(column, square))[0:1]


def outer(hid, hg, tok, scaled, in_grad, out_grad):
    out_grad[...] = mm(hid[...], scaled[...]).astype(BF)
    in_grad[...] = mm(hg[...], tok[...]).astype(BF)


def per_device(tokens, cotangent, gate_prob, experts_of, in_weight, out_weight):
    n = lax.axis_size("expert")
    slabs = n // EXPERTS
    count, width = tokens.shape
    ffn = in_weight.shape[0]
    cap = 5 * count // (4 * EXPERTS)
    chunk = width // PARTS
    rows = EXPERTS * SUB
    total = n * SUB
    anywhere = pl.BlockSpec(memory_space=pl.ANY)
    vmem = pl.BlockSpec(memory_space=pltpu.VMEM)
    dma = pltpu.SemaphoreType.DMA
    gate_grad, hid, hg, tok, scaled = pl.pallas_call(
        functools.partial(exchange, n, slabs, cap),
        out_shape=(
            jax.ShapeDtypeStruct((1, count), F32),
            jax.ShapeDtypeStruct((ffn, total), BF),
            jax.ShapeDtypeStruct((ffn, total), BF),
            jax.ShapeDtypeStruct((total, width), BF),
            jax.ShapeDtypeStruct((total, width), BF),
        ),
        in_specs=[anywhere, anywhere, vmem, vmem, anywhere, anywhere],
        out_specs=(vmem, vmem, vmem, anywhere, anywhere),
        scratch_shapes=[
            pltpu.VMEM((2 * count, width), BF),
            pltpu.VMEM((rows, chunk + 128), BF),
            pltpu.VMEM((PARTS, rows, chunk), BF),
            pltpu.VMEM((total, chunk + 128), BF),
            pltpu.VMEM((PARTS, total, chunk), BF),
            pltpu.VMEM((2, ffn, chunk), BF),
            pltpu.VMEM((2, ffn, chunk), BF),
            pltpu.VMEM((ffn, total), F32),
            pltpu.VMEM((ffn, total), F32),
            pltpu.VMEM((2, total, chunk), BF),
            pltpu.VMEM((2, total, chunk), BF),
            pltpu.VMEM((total // 128, 8, 128), F32),
            pltpu.VMEM((n, 8, 128), F32),
            dma((2,)),
            dma((2, 2)),
            dma((PARTS + 1,)),
            dma((PARTS + 1,)),
            dma((2, 2)),
            dma((2,)),
        ],
        compiler_params=pltpu.CompilerParams(
            collective_id=0, has_side_effects=True, vmem_limit_bytes=62 * 2**20
        ),
        name="exchange",
    )(
        tokens, cotangent, gate_prob.reshape(1, count), experts_of.reshape(1, count),
        in_weight, out_weight,
    )
    tile = math.gcd(ffn, 256)
    cols = min(width, width * 256 // total)
    left = pl.BlockSpec((tile, total), lambda c, i: (i, 0))
    right = pl.BlockSpec((total, cols), lambda c, i: (0, c))
    result = pl.BlockSpec((tile, cols), lambda c, i: (i, c))
    grad = jax.ShapeDtypeStruct((ffn, width), BF)
    in_grad, out_grad = pl.pallas_call(
        outer,
        grid=(width // cols, ffn // tile),
        out_shape=(grad, grad),
        in_specs=[left, left, right, right],
        out_specs=(result, result),
        compiler_params=pltpu.CompilerParams(vmem_limit_bytes=56 * 2**20),
        name="outer",
    )(hid, hg, tok, scaled)
    return (gate_grad.reshape(count), in_grad, out_grad)


def solution(mesh):
    return jax.shard_map(
        per_device,
        mesh=mesh,
        in_specs=(
            P(("groups", "expert"), None),
            P(("groups", "expert"), None),
            P(("groups", "expert")),
            P(("groups", "expert"), None),
            P("expert", None),
            P("expert", None),
        ),
        out_specs=(
            P(("groups", "expert")),
            P(("groups", "expert"), None),
            P(("groups", "expert"), None),
        ),
        check_vma=False,
    )
```

time: 168 us -> 96 us (0.57)
  Pallas kernels: 0 us -> 93.9 us
  waiting for transfers between devices: 69.3 us -> 0 us
  matrix products: 48.9 us -> 0 us
  starting transfers between devices: 33.6 us -> 0 us
  local copies, waits for them, and re-layouts: 9.63 us -> 1.17 us
  other arithmetic: 5.17 us -> 0 us
    pallas_call x0 -> x2, Pallas kernels: none -> 93.9 us  [the longest x1 76.7 us: per_device(): pl.pallas_call(functools.partial(exchange, n, slabs, cap), out_shape=(jax...]
    all_to_all x4 -> x0, waiting for transfers between devices: 69.3 us -> none  [the longest x1 36.8 us: per_device(): lax.all_to_all(spread(packed_tok), 'expert', split_axis=0, concat_axis=0,...]
    dot_general x6 -> x0, matrix products: 48.9 us -> none  [the longest x2 24.1 us: contract_last(): lax.dot_general(left, right, (((1,), (1,)), ((), ())), preferred_element_...]
    all_to_all x4 -> x0, starting transfers between devices: 33.6 us -> none  [the longest x1 11.2 us: per_device(): lax.all_to_all(spread(packed_grad), 'expert', split_axis=0, concat_axis=0...]
    another operation x2 -> x0, local copies, waits for them, and re-layouts: 4.17 us -> none  [spread(): return widened.reshape((devices,) + values.shape[1:])]
    reshape x2 -> x0, local copies, waits for them, and re-layouts: 3.96 us -> none  [the longest x1 2.61 us: per_device(): rows_grad = arrived_grad.reshape(devices * capacity, width)]
  transfers between devices with their start and end apart: 4 -> 0, of which waited for: 3 -> 0; matrix products, arithmetic and copies ran while one was open for 25% -> 0% of each run, Pallas kernels for 0% -> 0%
where the time goes in v1:
time: 96 us; the launch traced here: 95.8 us
  Pallas kernels  93.9 us (98%)
  local copies, waits for them, and re-layouts  1.17 us (1%)
    pallas_call x1, Pallas kernels, per_device(): pl.pallas_call(functools.partial(exchange, n, slabs, cap), out_shape=(jax...  76.7 us
    pallas_call x1, Pallas kernels, per_device(): pl.pallas_call(outer, grid=(width // cols, ffn // tile), out_shape=(grad,...  17.3 us

profile of v1, /device:TPU:0, one launch (start us, length us, event | category | flops | bytes accessed | tf_op | source)
XLA Modules:
  0.0 95.8 jit_solution(7539726289639747379)
XLA Ops:
  0.6 76.7 %exchange.1 = (f32[1,128]{1,0:T(1,128)}, bf16[2560,256]{1,0:T(8,128)(2,1)}, bf16[2560,256]{1,0:T(8,128)(2,1)}, bf16[256,4096]{1,0:T(8,128)(2,1)}, bf16[256,4096]{1,0:T(8,128)(2,1)}) custom-call(bf16[128,4096]{1,0:T(8,128)(2,1)} %tok.1, bf16[128,4096]{1,0:T(8,128)(2,1)} %cot.1, bf16[1,128]{1,0:T(2,128)(2,1)} %bitcast.3, s32[1,128]{1,0:T(1,128)} %bitcast.4, ...), custom_call_target="tpu_custom_call" | custom-call | tf_op jit(solution)/shard_map/exchange/pallas_call | solution.py:255
  77.3 17.3 %outer.1 = (bf16[2560,4096]{1,0:T(8,128)(2,1)}, bf16[2560,4096]{1,0:T(8,128)(2,1)}) custom-call(bf16[2560,256]{1,0:T(8,128)(2,1)} %get-tuple-element.11.hid, bf16[2560,256]{1,0:T(8,128)(2,1)} %get-tuple-element.12.hg, bf16[256,4096]{1,0:T(8,128)(2,1)} %get-tuple-element.13.tok, bf16[256,4096]{1,0:T(8,128)(2,1)} %get-tuple-element.14.scaled), custom_call_target="tpu_custom_call" | custom-call | tf_op jit(solution)/shard_map/outer/pallas_call | solution.py:301
  94.6 1.2 %copy.10 = f32[128]{0:T(128)} copy(f32[128]{0:T(128)} %bitcast.5) | data formatting | bytes 1024

commit v2 on v1

v2 whole, which is shorter than its diff:
```python
import functools
import math

import jax
import jax.numpy as jnp
from jax import lax
from jax.experimental import pallas as pl
from jax.experimental.pallas import tpu as pltpu
from jax.sharding import PartitionSpec as P

EXPERTS = 16
SUB = 16
PARTS = 4
MESH = pl.DeviceIdType.MESH
BF = jnp.bfloat16
F32 = jnp.float32


def contract_last(left, right):
    return lax.dot_general(
        left, right, (((1,), (1,)), ((), ())), preferred_element_type=F32
    )


def mm(left, right):
    return jnp.dot(left, right, preferred_element_type=F32)


def iota(shape, dim):
    return lax.broadcasted_iota(jnp.int32, shape, dim)


def hot(cond):
    return jnp.where(cond, 1.0, 0.0).astype(BF)


def exchange(
    n, slabs, cap,
    tok, cot, gate, who, w_in, w_out,
    gate_grad, hid_out, hg_out, tok_out, sc_out,
    stage, send_b, send_a, recv_b, recv_a, win, wout, pre, back,
    stg_tok, stg_sc, hid, hg, gate_s, gate_r, gate_cols, ret_s, ret_r,
    in_sem, w_sem, send_sem, recv_sem, out_sem, tile_sem, gate_sem, ret_sem,
):
    me = lax.axis_index("expert")
    count = tok.shape[0]
    chunk = stage.shape[1] // PARTS
    extra = SUB - cap
    rest = cap - extra
    rows = EXPERTS * SUB
    total = n * SUB
    ffn = w_in.shape[0]
    tile = math.gcd(ffn, 512)
    block = 256
    cut = chunk * 3 // 4
    steps = [(k, 0, chunk) for k in range(PARTS - 1)]
    steps += [(PARTS - 1, 0, cut), (PARTS - 1, cut, chunk - cut)]
    last = len(steps) - 1

    barrier = pltpu.get_barrier_semaphore()

    @pl.loop(1, n)
    def _(i):
        pl.semaphore_signal(
            barrier, inc=1, device_id={"expert": lax.rem(me + i, n)}, device_id_type=MESH
        )

    ins = [
        pltpu.make_async_copy(cot, stage.at[pl.ds(count, count)], in_sem.at[0]),
        pltpu.make_async_copy(tok, stage.at[pl.ds(0, count)], in_sem.at[1]),
    ]
    for c in ins:
        c.start()

    def weights(k):
        cols = pl.ds(k * chunk, chunk)
        return [
            pltpu.make_async_copy(w_in.at[:, cols], win.at[k % 2], w_sem.at[0, k % 2]),
            pltpu.make_async_copy(w_out.at[:, cols], wout.at[k % 2], w_sem.at[1, k % 2]),
        ]

    loads = [weights(k) for k in range(PARTS)]

    chosen = who[...]
    square = (count, count)
    chosen_col = jnp.transpose(jnp.broadcast_to(chosen.astype(F32), square)).astype(jnp.int32)
    earlier = (chosen_col == chosen) & (iota(square, 0) < iota(square, 1))
    place = jnp.sum(jnp.where(earlier, 1.0, 0.0), axis=0, keepdims=True)
    place_col = jnp.transpose(jnp.broadcast_to(place, square)).astype(jnp.int32)
    code = jnp.broadcast_to(chosen * SUB + place.astype(jnp.int32), (rows, count))
    row = iota((rows, count), 0)
    slot = row % SUB
    sel_tok = (code == row) & (slot < cap)
    sel_cot = (code == row - cap) & (slot >= cap)
    sel = jnp.concatenate([hot(sel_tok), hot(sel_cot)], axis=1)
    ins[0].wait()
    late = jnp.zeros((rows, chunk), F32)
    for q in range(PARTS):
        pick = hot((slot % PARTS == q) & (code == row - slot + extra + slot // PARTS))
        late = late + mm(pick, stage[pl.ds(count, count), pl.ds(q * chunk, chunk)])
    send_b[...] = late.astype(BF)
    ins[1].wait()

    pl.semaphore_wait(barrier, n - 1)

    def mine(ref, cols):
        return ref.at[pl.ds(pl.multiple_of(me * SUB, SUB), SUB), cols]

    def send(src, dst, cols, at):
        @pl.loop(1, n)
        def _(i):
            to = lax.rem(me + i, n)
            pltpu.make_async_remote_copy(
                src_ref=src.at[pl.ds(pl.multiple_of(to // slabs * SUB, SUB), SUB), cols],
                dst_ref=mine(dst, cols),
                send_sem=send_sem.at[at],
                recv_sem=recv_sem.at[at],
                device_id={"expert": to},
                device_id_type=MESH,
            ).start()

        dst[pl.ds(pl.multiple_of(me * SUB, SUB), SUB), cols] = src[
            pl.ds(pl.multiple_of(me // slabs * SUB, SUB), SUB), cols
        ]

    def finish(ref, sem):
        pltpu.make_async_copy(ref, ref, sem).wait()

    def others(dst, cols):
        return dst.at[pl.ds(0, total - SUB), cols]

    def send_rows(src, dst, pick, sem):
        @pl.loop(1, n)
        def _(i):
            to = lax.rem(me + i, n)
            pltpu.make_async_remote_copy(
                src_ref=src.at[pick(to)],
                dst_ref=dst.at[me],
                send_sem=sem.at[0],
                recv_sem=sem.at[1],
                device_id={"expert": to},
                device_id_type=MESH,
            ).start()

        dst[me] = src[pick(me)]

    whole = pl.ds(0, chunk)
    send(send_b, recv_b, whole, last + 1)
    for s, (k, start, size) in enumerate(steps):
        if start == 0:
            send_a[k] = mm(sel, stage[:, pl.ds(k * chunk, chunk)]).astype(BF)
        send(send_a.at[k], recv_a.at[k], pl.ds(start, size), s)
        if s == 0:
            gate_col = jnp.transpose(jnp.broadcast_to(gate[...].astype(F32), square))
            lane = iota((count, 128), 1) % SUB
            at_slot = (place_col == lane) & (lane < cap)
            for e in range(EXPERTS):
                picked = jnp.where(at_slot & (chosen_col == e), gate_col, 0.0)
                gate_s[e] = jnp.sum(picked, axis=0, keepdims=True)
            send_rows(gate_s, gate_r, lambda to: to // slabs, gate_sem)
            for i in range(2):
                for c in loads[i]:
                    c.start()

    per_tile = 128 // SUB
    finish(gate_r.at[pl.ds(0, n - 1)], gate_sem.at[1])
    lane = iota((1, 128), 1) // SUB
    gate_rows = []
    for h in range(total // 128):
        piece = jnp.zeros((1, 128), F32)
        for i in range(per_tile):
            piece = piece + jnp.where(lane == i, gate_r[h * per_tile + i], 0.0)
        gate_rows.append(piece)
        gate_cols[pl.ds(h * 128, 128), :] = jnp.transpose(jnp.broadcast_to(piece, (128, 128)))
    gate_row = jnp.concatenate(gate_rows, axis=1)
    finish(others(recv_b, whole), recv_sem.at[last + 1])

    def outs(k):
        cols = pl.ds(k * chunk, chunk)
        return [
            pltpu.make_async_copy(stg_tok.at[k % 2], tok_out.at[:, cols], out_sem.at[0, k % 2]),
            pltpu.make_async_copy(stg_sc.at[k % 2], sc_out.at[:, cols], out_sem.at[1, k % 2]),
        ]

    writes = [outs(k) for k in range(PARTS)]
    r0 = iota((block, block), 0)
    r1 = iota((block, block), 1)
    j = r0 % SUB
    keep = hot((r0 == r1) & (j < cap))
    first = hot((r1 == r0 + cap) & (j < extra))
    part_sum = jnp.zeros((8, total), F32)

    def tiles(i):
        at = pl.ds(pl.multiple_of(i * tile, tile), tile)
        return [
            pltpu.make_async_copy(hid.at[at], hid_out.at[at], tile_sem.at[0, i]),
            pltpu.make_async_copy(hg.at[at], hg_out.at[at], tile_sem.at[1, i]),
        ]

    for s, (k, start, size) in enumerate(steps):
        cols = pl.ds(start, size)
        if start == 0:
            for c in loads[k]:
                c.wait()
            if k >= 2:
                for c in writes[k - 2]:
                    c.wait()
        finish(others(recv_a.at[k], cols), recv_sem.at[s])
        second = hot((j >= extra) & (j < cap) & (r1 == r0 - j + (j - extra) * PARTS + k))

        @pl.loop(0, total // block)
        def _(b):
            at = pl.ds(pl.multiple_of(b * block, block), block)
            mixed = recv_a[k, at, cols]
            stg_tok[k % 2, at, cols] = mm(keep, mixed).astype(BF)
            grads = mm(first, mixed) + mm(second, recv_b[at, cols])
            recv_a[k, at, cols] = grads.astype(BF)
            stg_sc[k % 2, at, cols] = (gate_cols[at, :][:, 0:1] * grads).astype(BF)

        if start + size == chunk:
            for c in writes[k]:
                c.start()

        def step(i, acc):
            at = pl.ds(pl.multiple_of(i * tile, tile), tile)
            p = contract_last(win[k % 2, at, cols], stg_tok[k % 2, :, cols])
            g = contract_last(wout[k % 2, at, cols], recv_a[k, :, cols])
            if s > 0:
                p = p + pre[at, :]
                g = g + back[at, :]
            if s < last:
                pre[at, :] = p
                back[at, :] = g
                return acc
            hidden = jnp.maximum(p, 0.0).astype(BF)
            hid[at, :] = hidden
            hg[at, :] = jnp.where(p > 0, gate_row * g, 0.0).astype(BF)
            for c in tiles(i):
                c.start()
            share = hidden.astype(F32) * g
            return acc + jnp.sum(share.reshape(tile // 8, 8, total), axis=0)

        part_sum = lax.fori_loop(0, ffn // tile, step, part_sum)
        if start + size == chunk and k + 2 < PARTS:
            for c in loads[k + 2]:
                c.start()

    shares = jnp.sum(part_sum, axis=0, keepdims=True)
    for h in range(total // 128):
        ret_s[h] = shares[:, h * 128:(h + 1) * 128]

    send_rows(ret_s, ret_r, lambda to: to // per_tile, ret_sem)
    for k in range(PARTS - 2, PARTS):
        for c in writes[k]:
            c.wait()

    @pl.loop(0, ffn // tile)
    def _(i):
        for c in tiles(i):
            c.wait()

    for s, (k, start, size) in enumerate(steps):
        finish(others(recv_a.at[k], pl.ds(start, size)), send_sem.at[s])
    finish(others(recv_b, whole), send_sem.at[last + 1])
    finish(gate_r.at[pl.ds(0, n - 1)], gate_sem.at[0])
    for i in range(2):
        finish(ret_r.at[pl.ds(0, n - 1)], ret_sem.at[i])

    found = jnp.zeros((count, 128), F32)
    for d in range(n):
        found = found + jnp.where(chosen_col == d // slabs, ret_r[d], 0.0)
    own = iota((count, 128), 1) == place_col + SUB * lax.rem(me, per_tile)
    column = jnp.sum(jnp.where(own, found, 0.0), axis=1, keepdims=True)
    gate_grad[...] = jnp.transpose(jnp.broadcast_to(column, square))[0:1]


def outer(hid, hg, tok, scaled, gate_in, in_grad, out_grad, gate_out):
    gate_out[...] = gate_in[...]
    out_grad[...] = mm(hid[...], scaled[...]).astype(BF)
    in_grad[...] = mm(hg[...], tok[...]).astype(BF)


def per_device(tokens, cotangent, gate_prob, experts_of, in_weight, out_weight):
    n = lax.axis_size("expert")
    slabs = n // EXPERTS
    count, width = tokens.shape
    ffn = in_weight.shape[0]
    cap = 5 * count // (4 * EXPERTS)
    chunk = width // PARTS
    rows = EXPERTS * SUB
    total = n * SUB
    anywhere = pl.BlockSpec(memory_space=pl.ANY)
    vmem = pl.BlockSpec(memory_space=pltpu.VMEM)
    dma = pltpu.SemaphoreType.DMA
    gate_grad, hid, hg, tok, scaled = pl.pallas_call(
        functools.partial(exchange, n, slabs, cap),
        out_shape=(
            jax.ShapeDtypeStruct((1, count), F32),
            jax.ShapeDtypeStruct((ffn, total), BF),
            jax.ShapeDtypeStruct((ffn, total), BF),
            jax.ShapeDtypeStruct((total, width), BF),
            jax.ShapeDtypeStruct((total, width), BF),
        ),
        in_specs=[anywhere, anywhere, vmem, vmem, anywhere, anywhere],
        out_specs=(vmem,) + (anywhere,) * 4,
        scratch_shapes=[
            pltpu.VMEM((2 * count, width), BF),
            pltpu.VMEM((rows, chunk), BF),
            pltpu.VMEM((PARTS, rows, chunk), BF),
            pltpu.VMEM((total, chunk), BF),
            pltpu.VMEM((PARTS, total, chunk), BF),
            pltpu.VMEM((2, ffn, chunk), BF),
            pltpu.VMEM((2, ffn, chunk), BF),
            pltpu.VMEM((ffn, total), F32),
            pltpu.VMEM((ffn, total), F32),
            pltpu.VMEM((2, total, chunk), BF),
            pltpu.VMEM((2, total, chunk), BF),
            pltpu.VMEM((ffn, total), BF),
            pltpu.VMEM((ffn, total), BF),
            pltpu.VMEM((EXPERTS, 1, 128), F32),
            pltpu.VMEM((n, 1, 128), F32),
            pltpu.VMEM((total, 128), F32),
            pltpu.VMEM((total // 128, 1, 128), F32),
            pltpu.VMEM((n, 1, 128), F32),
            dma((2,)),
            dma((2, 2)),
            dma((PARTS + 2,)),
            dma((PARTS + 2,)),
            dma((2, 2)),
            dma((2, ffn // math.gcd(ffn, 512))),
            dma((2,)),
            dma((2,)),
        ],
        compiler_params=pltpu.CompilerParams(
            collective_id=0, has_side_effects=True, vmem_limit_bytes=(42 if total <= 256 else 62) * 2**20
        ),
        name="exchange",
    )(
        tokens, cotangent, gate_prob.reshape(1, count), experts_of.reshape(1, count),
        in_weight, out_weight,
    )
    tile = math.gcd(ffn, 256)
    cols = min(width, width * 256 // total)
    left = pl.BlockSpec((tile, total), lambda c, i: (i, 0))
    right = pl.BlockSpec((total, cols), lambda c, i: (0, c))
    result = pl.BlockSpec((tile, cols), lambda c, i: (i, c))
    small = pl.BlockSpec((1, count), lambda c, i: (0, 0))
    grad = jax.ShapeDtypeStruct((ffn, width), BF)
    in_grad, out_grad, gate_grad = pl.pallas_call(
        outer,
        grid=(width // cols, ffn // tile),
        out_shape=(grad, grad, jax.ShapeDtypeStruct((1, count), F32)),
        in_specs=[left, left, right, right, small],
        out_specs=(result, result, small),
        compiler_params=pltpu.CompilerParams(vmem_limit_bytes=(28 if total <= 256 else 56) * 2**20),
        name="outer",
    )(hid, hg, tok, scaled, gate_grad)
    return (gate_grad.reshape(count), in_grad, out_grad)


def solution(mesh):
    return jax.shard_map(
        per_device,
        mesh=mesh,
        in_specs=(
            P(("groups", "expert"), None),
            P(("groups", "expert"), None),
            P(("groups", "expert")),
            P(("groups", "expert"), None),
            P("expert", None),
            P("expert", None),
        ),
        out_specs=(
            P(("groups", "expert")),
            P(("groups", "expert"), None),
            P(("groups", "expert"), None),
        ),
        check_vma=False,
    )
```

time: 96 us -> 95.4 us (level)
  Pallas kernels: 93.9 us -> 90.8 us
  local copies, waits for them, and re-layouts: 1.17 us -> 3.75 us
    pallas_call x1, Pallas kernels: 76.7 us -> 74 us  [per_device(): pl.pallas_call(functools.partial(exchange, n, slabs, cap), out_shape=(jax...]
    unnamed x1 -> x8, local copies, waits for them, and re-layouts: 1.17 us -> 3.75 us
where the time goes in v2:
time: 95.4 us; the launch traced here: 95.2 us
  Pallas kernels  90.8 us (95%)
  local copies, waits for them, and re-layouts  3.75 us (4%)
    pallas_call x1, Pallas kernels, per_device(): pl.pallas_call(functools.partial(exchange, n, slabs, cap), out_shape=(jax...  74 us
    pallas_call x1, Pallas kernels, per_device(): pl.pallas_call(outer, grid=(width // cols, ffn // tile), out_shape=(grad,...  16.8 us
    unnamed x8, local copies, waits for them, and re-layouts  3.75 us

profile of v2, /device:TPU:0, one launch (start us, length us, event | category | flops | bytes accessed | tf_op | source)
XLA Modules:
  0.0 95.2 jit_solution(17551530570744600393)
XLA Ops:
  0.6 0.0 copy-start
  0.6 1.2 %copy-done = bf16[128,4096]{1,0:T(8,128)(2,1)S(1)} copy-done((bf16[128,4096]{1,0:T(8,128)(2,1)S(1)}, bf16[128,4096]{1,0:T(8,128)(2,1)}, u32[]{:S(2)}) %copy-start) | copy-done | bytes 1048600
  1.9 0.0 copy-start.1
  1.9 1.2 %copy-done.1 = bf16[128,4096]{1,0:T(8,128)(2,1)S(1)} copy-done((bf16[128,4096]{1,0:T(8,128)(2,1)S(1)}, bf16[128,4096]{1,0:T(8,128)(2,1)}, u32[]{:S(2)}) %copy-start.1) | copy-done | bytes 1048600
  3.1 0.0 copy-start.2
  3.1 0.7 copy-done.2
  3.7 0.0 copy-start.3
  3.7 0.7 copy-done.3
  4.4 74.0 %exchange.1 = (f32[1,128]{1,0:T(1,128)S(1)}, bf16[2560,256]{1,0:T(8,128)(2,1)S(1)}, bf16[2560,256]{1,0:T(8,128)(2,1)S(1)}, bf16[256,4096]{1,0:T(8,128)(2,1)S(1)}, bf16[256,4096]{1,0:T(8,128)(2,1)S(1)}) custom-call(bf16[128,4096]{1,0:T(8,128)(2,1)S(1)} %copy-done, bf16[128,4096]{1,0:T(8,128)(2,1)S(1)} %copy-done.1, bf16[1,128]{1,0:T(2,128)(2,1)S(1)} %bitcast.3, ...), custom_call_target="tpu_custom_call" | custom-call | tf_op jit(solution)/shard_map/exchange/pallas_call | solution.py:295
  78.4 16.8 %outer.1 = (bf16[2560,4096]{1,0:T(8,128)(2,1)}, bf16[2560,4096]{1,0:T(8,128)(2,1)}, f32[1,128]{1,0:T(1,128)}) custom-call(bf16[2560,256]{1,0:T(8,128)(2,1)S(1)} %get-tuple-element.11.hid, bf16[2560,256]{1,0:T(8,128)(2,1)S(1)} %get-tuple-element.12.hg, bf16[256,4096]{1,0:T(8,128)(2,1)S(1)} %get-tuple-element.13.tok, ...), custom_call_target="tpu_custom_call" | custom-call | tf_op jit(solution)/shard_map/outer/pallas_call | solution.py:349
Async XLA Ops:
  0.6 1.2 %copy-start = (bf16[128,4096]{1,0:T(8,128)(2,1)S(1)}, bf16[128,4096]{1,0:T(8,128)(2,1)}, u32[]{:S(2)}) copy-start(bf16[128,4096]{1,0:T(8,128)(2,1)} %tok.1) | copy-start | bytes 3145732
  1.9 1.2 %copy-start.1 = (bf16[128,4096]{1,0:T(8,128)(2,1)S(1)}, bf16[128,4096]{1,0:T(8,128)(2,1)}, u32[]{:S(2)}) copy-start(bf16[128,4096]{1,0:T(8,128)(2,1)} %cot.1) | copy-start | bytes 3145732
  3.1 0.7 copy-start.2
  3.7 0.7 copy-start.3
